TPU v7x, 32 devices: a whole 2x2x4 slice. The times are simulated.
32 devices in a mesh: lat: 4 (over x, core), lon: 8 (over z, y).
Axes of the slice: x: 2, y: 2, z: 4, core: 2. Of those that a mesh axis runs over, the one named last changes fastest.
Arguments:
- queries: bfloat16 [8192, 1024], P(('lat', 'lon')), may hold values from -6 to 6
- gain: bfloat16 [1024], replicated, may hold values from 0.099609375 to 1.8984375
- w_query: bfloat16 [1024, 1024], P('lon'), may hold values from -0.1875 to 0.1875
- w_out: bfloat16 [1024, 1024], P(None, 'lon'), may hold values from -0.75 to 0.75
- kv_cache: bfloat16 [2, 8, 256, 1024], P(None, 'lat'), may hold values from -60 to 60
- nbr_lists: int32 [32, 4], P(('lat', 'lon')), may hold values from 0 to 7, as said below
- counts: int32 [32], P(('lat', 'lon')), may hold values from 1 to 4, as said below
Outputs:
- decoded: bfloat16 [8192, 1024], P(('lat', 'lon'))
Inputs may be any that keep to these rules, and one draw needn't show every extreme that they name: `nbr_lists`: query block b lies in band b // 8; band k holds latent blocks k * 2 to (k+1) * 2 - 1. Entries of b's list lie in its band or the bands beside it; its first counts[b] entries differ, the others repeat entry 0. `counts`: query blocks of the first and last band have 4 valid slots.
All inputs are finite; a program needn't handle non-finite values.
Results may differ from a plain program's by a relative error of at most 0.007.
The roundings to bfloat16 on the way count: a program that leaves them out, or rounds other values in their place, can miss the bound.
Values may be sent and summed in bfloat16 or wider, within the bound.
A program may use at most 64 MiB of HBM per device.

v0:
```python
import jax
import jax.numpy as jnp
from jax import lax
from jax.sharding import PartitionSpec as P

H = 16
HD = 64
BLOCK_TOKENS = 256


def padded(array, sides, width):
    for axis, dim in sides:
        devices, length = (lax.axis_size(axis), array.shape[dim])
        up = [(i, (i + 1) % devices) for i in range(devices - 1)]
        down = [(j, i) for i, j in up]
        last = lax.slice_in_dim(array, length - width, length, axis=dim)
        initial = lax.slice_in_dim(array, 0, width, axis=dim)
        before = lax.ppermute(last, axis, up)
        after = lax.ppermute(initial, axis, down)
        array = jnp.concatenate([before, array, after], axis=dim)
    return array


def on_device(queries, gain, w_query, w_out, kv_cache, nbr_lists, counts):
    rows = queries.astype(jnp.float32)
    rowwise_scale = lax.rsqrt(jnp.mean(rows * rows, axis=1, keepdims=True) + 1e-05)
    normed = (rows * rowwise_scale * gain.astype(jnp.float32)[None, :]).astype(jnp.bfloat16)
    row_count = queries.shape[0]
    query_count = row_count // BLOCK_TOKENS
    projected = jnp.dot(
        normed,
        lax.all_gather(w_query, "lon", axis=0, tiled=True),
        preferred_element_type=jnp.float32,
    )
    query = (projected * HD ** (-0.5)).astype(jnp.bfloat16)
    q_heads = query.reshape(query_count, BLOCK_TOKENS, H, HD)
    lat_index = lax.axis_index("lat")
    blocks_here = kv_cache.shape[1]
    window = padded(kv_cache, (("lat", 1),), blocks_here)
    key_window = window[0].reshape(3 * blocks_here, BLOCK_TOKENS, H, HD)
    value_window = window[1].reshape(3 * blocks_here, BLOCK_TOKENS, H, HD)
    local_lists = nbr_lists - (lat_index - 1) * blocks_here

    def update(state, scores, is_live, value_rows, value_form):
        best, total_sum, running = state
        peak = jnp.max(scores, axis=3)
        new_best = jnp.where(is_live[:, None, None], jnp.maximum(best, peak), best)
        rescale = jnp.exp(best - new_best)
        expo = jnp.where(is_live[:, None, None, None], jnp.exp(scores - new_best[..., None]), 0.0)
        total_sum = total_sum * rescale + jnp.sum(expo, axis=3)
        mixed = jnp.einsum(
            value_form, expo.astype(jnp.bfloat16), value_rows, preferred_element_type=jnp.float32
        )
        running = running * rescale[..., None] + mixed
        return (new_best, total_sum, running)

    start_state = (
        jnp.full((query_count, BLOCK_TOKENS, H), -1e30, jnp.float32),
        jnp.zeros((query_count, BLOCK_TOKENS, H), jnp.float32),
        jnp.zeros((query_count, BLOCK_TOKENS, H, HD), jnp.float32),
    )

    def listed_step(slot_index, state):
        picked = lax.dynamic_slice_in_dim(local_lists, slot_index, 1, 1)[:, 0]
        key_rows = jnp.take(key_window, picked, axis=0)
        value_rows = jnp.take(value_window, picked, axis=0)
        scores = jnp.einsum(
            "bqhd,bkhd->bqhk", q_heads, key_rows, preferred_element_type=jnp.float32
        )
        return update(state, scores, slot_index < counts, value_rows, "bqhk,bkhd->bqhd")

    final_state = lax.fori_loop(0, jnp.max(counts), listed_step, start_state)
    attended = (
        (final_state[2] / final_state[1][..., None]).reshape(row_count, H * HD).astype(jnp.bfloat16)
    )
    decoded = jnp.dot(
        attended,
        lax.all_gather(w_out, "lon", axis=1, tiled=True),
        preferred_element_type=jnp.float32,
    )
    return decoded.astype(jnp.bfloat16)


def solution(mesh):
    placed = (
        P(("lat", "lon"), None),
        P(),
        P("lon", None),
        P(None, "lon"),
        P(None, "lat", None, None),
        P(("lat", "lon"), None),
        P(("lat", "lon")),
    )
    return jax.shard_map(
        on_device, mesh=mesh, in_specs=placed, out_specs=P(("lat", "lon"), None), check_vma=False
    )
```

profile of v0, /device:TPU:1, one launch (start us, length us, event | category | flops | bytes accessed | tf_op | source)
XLA Modules:
  0.0 121.9 jit_solution(10355688768124419691)
XLA Ops:
  6.5 0.0 copy-start
  6.5 0.0 all-gather.3.cloned.1.call-start
  6.5 0.7 all-gather.3.cloned.1.call-update
  7.3 0.0 all-gather.5.cloned.1.call-start
  7.3 4.5 %collective-permute-start = (bf16[2,2,256,1024]{3,2,1,0:T(8,128)(2,1)}, bf16[2,2,256,1024]{3,2,1,0:T(8,128)(2,1)}, u32[]{:S(2)}, u32[]{:S(2)}) collective-permute-start(bf16[2,2,256,1024]{3,2,1,0:T(8,128)(2,1)} %param.15), channel_id=1, source_target_pairs={{0,8},{8,16},{16,24},{1,9},{9,17},{17,25},{2,10},{10,18},{18,26},{... | collective-permute-start | bytes 6291464 | tf_op jit(solution)/shard_map/ppermute | solution.py:18
  11.8 1.9 %collective-permute-start.1 = (bf16[2,2,256,1024]{3,2,1,0:T(8,128)(2,1)}, bf16[2,2,256,1024]{3,2,1,0:T(8,128)(2,1)}, u32[]{:S(2)}, u32[]{:S(2)}) collective-permute-start(bf16[2,2,256,1024]{3,2,1,0:T(8,128)(2,1)} %param.15), channel_id=1, source_target_pairs={{8,0},{16,8},{24,16},{9,1},{17,9},{25,17},{10,2},{18,10},{26,18},{... | collective-permute-start | bytes 6291464 | tf_op jit(solution)/shard_map/ppermute | solution.py:19
  13.8 0.0 all-gather.5.cloned.1.call-update
  13.8 0.7 convert_element_type.25
  14.5 1.2 %fusion.35 = f32[256]{0:T(256)S(1)} fusion(bf16[256,1024]{1,0:T(8,128)(2,1)} %param.11), kind=kLoop, calls=%fused_computation.40 | loop fusion | flops 786176 | bytes 525312 | tf_op jit(solution)/shard_map/reduce_sum | solution.py:26
  15.7 0.7 broadcast_subtract_fusion
  16.4 18.7 %collective-permute-done = bf16[2,2,256,1024]{3,2,1,0:T(8,128)(2,1)} collective-permute-done((bf16[2,2,256,1024]{3,2,1,0:T(8,128)(2,1)}, bf16[2,2,256,1024]{3,2,1,0:T(8,128)(2,1)}, u32[]{:S(2)}, u32[]{:S(2)}) %collective-permute-start) | collective-permute-done | bytes 2097184 | tf_op jit(solution)/shard_map/ppermute | solution.py:18
  35.1 1.8 %constant_dynamic-update-slice_fusion.2 = bf16[2,6,256,1024]{3,2,1,0:T(8,128)(2,1)S(1)} fusion(bf16[2,2,256,1024]{3,2,1,0:T(8,128)(2,1)} %collective-permute-done), kind=kLoop, calls=%fused_computation.48 | loop fusion | bytes 4194304
  36.9 0.0 copy-done
  36.9 0.2 constant_dynamic-update-slice_fusion.1
  37.0 2.4 %collective-permute-done.1 = bf16[2,2,256,1024]{3,2,1,0:T(8,128)(2,1)} collective-permute-done((bf16[2,2,256,1024]{3,2,1,0:T(8,128)(2,1)}, bf16[2,2,256,1024]{3,2,1,0:T(8,128)(2,1)}, u32[]{:S(2)}, u32[]{:S(2)}) %collective-permute-start.1) | collective-permute-done | bytes 2097184 | tf_op jit(solution)/shard_map/ppermute | solution.py:19
  39.5 1.8 %constant_dynamic-update-slice_fusion = bf16[2,6,256,1024]{3,2,1,0:T(8,128)(2,1)S(1)} fusion(bf16[2,6,256,1024]{3,2,1,0:T(8,128)(2,1)S(1)} %constant_dynamic-update-slice_fusion.1, bf16[2,2,256,1024]{3,2,1,0:T(8,128)(2,1)} %collective-permute-done.1), kind=kLoop, calls=%fused_computation.46 | loop fusion | bytes 4194304 | tf_op jit(solution)/shard_map/concatenate | solution.py:20
  41.3 2.7 %fusion.41 = (bf16[1,6,256,1024]{3,2,1,0:T(8,128)(2,1)S(1)}, bf16[1,6,256,1024]{3,2,1,0:T(8,128)(2,1)}) fusion(bf16[2,6,256,1024]{3,2,1,0:T(8,128)(2,1)S(1)} %constant_dynamic-update-slice_fusion), kind=kLoop, calls=%fused_computation.51 | loop fusion | bytes 12582912 | tf_op jit(solution)/shard_map/slice | solution.py:41
  44.0 4.7 %copy.13 = bf16[1,6,256,1024]{2,3,1,0:T(8,128)(2,1)} copy(bf16[1,6,256,1024]{3,2,1,0:T(8,128)(2,1)} %get-tuple-element.108) | data formatting | bytes 6291456 | tf_op jit(solution)/shard_map/slice | solution.py:40
  48.7 2.8 %copy.15 = bf16[1,6,256,1024]{2,3,1,0:T(8,128)(2,1)} copy(bf16[1,6,256,1024]{3,2,1,0:T(8,128)(2,1)S(1)} %get-tuple-element.107) | data formatting | bytes 6291456 | tf_op jit(solution)/shard_map/slice | solution.py:41
  51.5 8.3 %all-gather.3.cloned.1.call-done = bf16[1024,1024]{1,0:T(8,128)(2,1)} async-done(((bf16[128,1024]{1,0:T(8,128)(2,1)}), bf16[1024,1024]{1,0:T(8,128)(2,1)}) %all-gather.3.cloned.1.call-update) | async-done | bytes 2097168 | tf_op jit(solution)/shard_map/all_gather | solution.py:32
  59.8 2.5 %fusion.34 = bf16[256,1024]{1,0:T(8,128)(2,1)S(1)} fusion(bf16[1024,1024]{1,0:T(8,128)(2,1)} %all-gather.3.cloned.1.call-done, bf16[256,1024]{1,0:T(8,128)(2,1)} %param.11, f32[1024]{0:T(1024)S(1)} %convert_element_type.25, f32[256]{0:T(256)S(1)} %add_rsqrt_fusion), kind=kOutput, calls=%fused_computation.39 | convolution fusion | flops 538443776 | bytes 3150848 | tf_op jit(solution)/shard_map/dot_general | solution.py:30
  62.3 0.2 copy.14
  62.5 0.1 broadcast_in_dim.49
  62.6 25.9 %while.15 = (s32[]{:T(128)}, f32[1,256,16]{1,2,0:T(8,128)S(1)}, f32[1,256,16]{1,2,0:T(8,128)S(1)}, f32[1,256,16,64]{1,3,2,0:T(8,128)S(1)}, s32[]{:T(128)}, /*ind...) while((s32[]{:T(128)}, f32[1,256,16]{1,2,0:T(8,128)S(1)}, ...), condition=%wide.region_4.0_spmd, body=%wide.region_1.5_spmd.sunk | while | flops 276840448 | bytes 16517893 | solution.py:72
  63.3 0.6 constant_dynamic-slice_fusion.2
  65.8 1.8 %bitcast_reduce_fusion.2 = (f32[256,16]{0,1:T(8,128)S(1)}, f32[16,256,256]{2,1,0:T(8,128)S(1)}) fusion(bf16[1,256,16,64]{1,3,2,0:T(8,128)(2,1)S(1)} %get-tuple-element.219, bf16[6,256,16,64]{1,3,2,0:T(8,128)(2,1)} %get-tuple-element.218, s32[]{:T(128)} %bitcast.97, pred[]{:T(512)} %bitcast.98), kind=kOutput, calls=%fused_computation.1.clone.1 | convolution fusion | flops 135524352 | bytes 5260288 | tf_op jit(solution)/shard_map/while/body/bqhd,bkhd->bqhk/dot_general | solution.py:67
  68.3 2.0 %fusion.54 = f32[1,256,16,64]{1,3,2,0:T(8,128)S(1)} fusion(f32[16,256,256]{2,1,0:T(8,128)S(1)} %get-tuple-element.177, f32[256,16]{0,1:T(8,128)S(1)} %bitcast.105, pred[]{:T(512)} %bitcast.100, f32[1,256,16,64]{1,3,2,0:T(8,128)S(1)} %get-tuple-element.198, bf16[6,256,16,64]{1,3,2,0:T(8,128)(2,1)} %get-tuple-element.220, s32[]{:T(128)} %bitcast.97, ...), kind=kOutput, calls=%fused_computation.12.clone.1 | convolution fusion | flops 138149888 | bytes 6850048 | tf_op jit(solution)/shard_map/while/body/bqhk,bkhd->bqhd/dot_general | solution.py:51
  70.3 0.7 fusion.53
  71.7 0.6 constant_dynamic-slice_fusion.2
  74.2 1.8 %bitcast_reduce_fusion.2 = (f32[256,16]{0,1:T(8,128)S(1)}, f32[16,256,256]{2,1,0:T(8,128)S(1)}) fusion(bf16[1,256,16,64]{1,3,2,0:T(8,128)(2,1)S(1)} %get-tuple-element.219, bf16[6,256,16,64]{1,3,2,0:T(8,128)(2,1)} %get-tuple-element.218, s32[]{:T(128)} %bitcast.97, pred[]{:T(512)} %bitcast.98), kind=kOutput, calls=%fused_computation.1.clone.1 | convolution fusion | flops 135524352 | bytes 5260288 | tf_op jit(solution)/shard_map/while/body/bqhd,bkhd->bqhk/dot_general | solution.py:67
  76.7 2.0 %fusion.54 = f32[1,256,16,64]{1,3,2,0:T(8,128)S(1)} fusion(f32[16,256,256]{2,1,0:T(8,128)S(1)} %get-tuple-element.177, f32[256,16]{0,1:T(8,128)S(1)} %bitcast.105, pred[]{:T(512)} %bitcast.100, f32[1,256,16,64]{1,3,2,0:T(8,128)S(1)} %get-tuple-element.198, bf16[6,256,16,64]{1,3,2,0:T(8,128)(2,1)} %get-tuple-element.220, s32[]{:T(128)} %bitcast.97, ...), kind=kOutput, calls=%fused_computation.12.clone.1 | convolution fusion | flops 138149888 | bytes 6850048 | tf_op jit(solution)/shard_map/while/body/bqhk,bkhd->bqhd/dot_general | solution.py:51
  78.7 0.7 fusion.53
  80.1 0.6 constant_dynamic-slice_fusion.2
  82.7 1.8 %bitcast_reduce_fusion.2 = (f32[256,16]{0,1:T(8,128)S(1)}, f32[16,256,256]{2,1,0:T(8,128)S(1)}) fusion(bf16[1,256,16,64]{1,3,2,0:T(8,128)(2,1)S(1)} %get-tuple-element.219, bf16[6,256,16,64]{1,3,2,0:T(8,128)(2,1)} %get-tuple-element.218, s32[]{:T(128)} %bitcast.97, pred[]{:T(512)} %bitcast.98), kind=kOutput, calls=%fused_computation.1.clone.1 | convolution fusion | flops 135524352 | bytes 5260288 | tf_op jit(solution)/shard_map/while/body/bqhd,bkhd->bqhk/dot_general | solution.py:67
  85.1 2.0 %fusion.54 = f32[1,256,16,64]{1,3,2,0:T(8,128)S(1)} fusion(f32[16,256,256]{2,1,0:T(8,128)S(1)} %get-tuple-element.177, f32[256,16]{0,1:T(8,128)S(1)} %bitcast.105, pred[]{:T(512)} %bitcast.100, f32[1,256,16,64]{1,3,2,0:T(8,128)S(1)} %get-tuple-element.198, bf16[6,256,16,64]{1,3,2,0:T(8,128)(2,1)} %get-tuple-element.220, s32[]{:T(128)} %bitcast.97, ...), kind=kOutput, calls=%fused_computation.12.clone.1 | convolution fusion | flops 138149888 | bytes 6850048 | tf_op jit(solution)/shard_map/while/body/bqhk,bkhd->bqhd/dot_general | solution.py:51
  87.1 0.7 fusion.53
  88.5 0.1 divide_convert_fusion
  88.6 23.3 %all-gather.5.cloned.1.call-done = bf16[1024,1024]{1,0:T(8,128)(2,1)} async-done(((bf16[1024,128]{1,0:T(8,128)(2,1)}), bf16[1024,1024]{1,0:T(8,128)(2,1)}) %all-gather.5.cloned.1.call-update) | async-done | bytes 2097168 | tf_op jit(solution)/shard_map/all_gather | solution.py:78
  111.9 3.1 %convolution_convert_fusion = bf16[256,1024]{1,0:T(8,128)(2,1)} fusion(bf16[256,1024]{0,1:T(8,128)(2,1)S(1)} %bitcast.107, bf16[1024,1024]{1,0:T(8,128)(2,1)} %all-gather.5.cloned.1.call-done), kind=kOutput, calls=%fused_computation.38 | convolution fusion | flops 537133056 | bytes 3145728 | tf_op jit(solution)/shard_map/dot_general | solution.py:76
  (12 shorter events, 0.1 us)
Async XLA Ops:
  6.5 30.3 %copy-start = (bf16[2,2,256,1024]{3,2,1,0:T(8,128)(2,1)S(1)}, bf16[2,2,256,1024]{3,2,1,0:T(8,128)(2,1)}, u32[]{:S(2)}) copy-start(bf16[2,2,256,1024]{3,2,1,0:T(8,128)(2,1)} %param.15) | copy-start | bytes 6291460
  6.5 53.2 %all-gather.3.cloned.1.call-start = ((), (), s32[]{:S(2)}) async-start(), calls=%async_computation | async-start | bytes 2359296 | tf_op jit(solution)/shard_map/all_gather | solution.py:32
  7.3 104.7 %all-gather.5.cloned.1.call-start = ((), (), s32[]{:S(2)}) async-start(), calls=%async_computation.1 | async-start | bytes 2359296 | tf_op jit(solution)/shard_map/all_gather | solution.py:78
  7.3 27.8 %collective-permute-start = (bf16[2,2,256,1024]{3,2,1,0:T(8,128)(2,1)}, bf16[2,2,256,1024]{3,2,1,0:T(8,128)(2,1)}, u32[]{:S(2)}, u32[]{:S(2)}) collective-permute-start(bf16[2,2,256,1024]{3,2,1,0:T(8,128)(2,1)} %param.15), channel_id=1, source_target_pairs={{0,8},{8,16},{16,24},{1,9},{9,17},{17,25},{2,10},{10,18},{18,26},{... | collective-permute-start | bytes 6291464 | tf_op jit(solution)/shard_map/ppermute | solution.py:18
  11.8 27.7 %collective-permute-start.1 = (bf16[2,2,256,1024]{3,2,1,0:T(8,128)(2,1)}, bf16[2,2,256,1024]{3,2,1,0:T(8,128)(2,1)}, u32[]{:S(2)}, u32[]{:S(2)}) collective-permute-start(bf16[2,2,256,1024]{3,2,1,0:T(8,128)(2,1)} %param.15), channel_id=1, source_target_pairs={{8,0},{16,8},{24,16},{9,1},{17,9},{25,17},{10,2},{18,10},{26,18},{... | collective-permute-start | bytes 6291464 | tf_op jit(solution)/shard_map/ppermute | solution.py:19
Sparse Core Ops, SparseCore 0:
  9.5 50.2 all-gather.2
  61.8 50.0 all-gather.4
where the time goes:
time: 124 us; the launch traced here: 122 us
  waiting for transfers between devices  53.5 us (43%)
  matrix products  17 us (14%)
  local copies, waits for them, and re-layouts  16.2 us (13%)
  between operations  13.5 us (11%)
  loops' own time  10.4 us (8%)
  starting transfers between devices  6.47 us (5%)
  other arithmetic  4.89 us (4%)
    all_gather x1, waiting for transfers between devices, on_device(): lax.all_gather(w_out, 'lon', axis=1, tiled=True)  23.3 us
    ppermute x1, waiting for transfers between devices, padded(): before = lax.ppermute(last, axis, up)  18.7 us
    another operation x1, loops' own time, on_device(): final_state = lax.fori_loop(0, jnp.max(counts), listed_step, start_state)  10.4 us
    all_gather x1, waiting for transfers between devices, on_device(): lax.all_gather(w_query, 'lon', axis=0, tiled=True)  8.27 us
    dot_general x3, matrix products, update(): jnp.einsum(value_form, expo.astype(jnp.bfloat16), value_rows, preferred_e...  5.93 us
    slice x2, local copies, waits for them, and re-layouts, on_device(): value_window = window[1].reshape(3 * blocks_here, BLOCK_TOKENS, H, HD)  5.54 us
    dot_general x3, matrix products, listed_step(): jnp.einsum('bqhd,bkhd->bqhk', q_heads, key_rows, preferred_element_type=j...  5.43 us
    slice x1, local copies, waits for them, and re-layouts, on_device(): key_window = window[0].reshape(3 * blocks_here, BLOCK_TOKENS, H, HD)  4.7 us
  transfers between devices with their start and end apart: 4, of which 4 were waited for; matrix products, arithmetic and copies ran while one was open for 29% of the time, Pallas kernels for 0%

commit v1 on v0

v1 whole, which is shorter than its diff:
```python
import functools

import jax
import jax.numpy as jnp
from jax import lax
from jax.experimental import pallas as pl
from jax.experimental.pallas import tpu as pltpu
from jax.sharding import PartitionSpec as P

H = 16
HD = 64
PAIR = 2 * HD
BLOCK_TOKENS = 256
MESH = pl.DeviceIdType.MESH
LOW = -1e30


def remote(src, dst, send_sem, recv_sem, device):
    return pltpu.make_async_remote_copy(
        src_ref=src, dst_ref=dst, send_sem=send_sem, recv_sem=recv_sem, device_id=device, device_id_type=MESH
    )


def kernel(
    n_lat, n_z, n_y,
    lists_ref, counts_ref, queries_ref, gain_ref, wq_ref, wo_ref, kv_ref,
    out_ref,
    wq_all, wo_all, kv_own, kv_chip, kv_far, normed, heads, best, total, running, attended,
    own_sems, kv_send, kv_recv, wq_z, wq_y, wq_core, wq_recv, wo_z, wo_y, wo_core, wo_recv,
):
    n_lon = n_z * n_y
    lat, lon = lax.axis_index("lat"), lax.axis_index("lon")
    z, y, core = lon // n_y, lon % n_y, lat % 2
    mate = lat + 1 - 2 * core
    far = lat - 1 + 2 * core
    has_far = jnp.logical_and(far >= 0, far < n_lat)
    far_safe = jnp.clip(far, 0, n_lat - 1)
    pairs = H // 2
    rows = queries_ref.shape[0]
    depth, columns = wq_ref.shape[0], wo_ref.shape[1]
    half_q, half_o = depth // 2, wo_ref.shape[0] // 2
    blocks = kv_ref.shape[1]

    own_copies = [
        pltpu.make_async_copy(wq_ref, wq_all.at[pl.ds(pl.multiple_of(lon * depth, depth), depth)], own_sems.at[0]),
        pltpu.make_async_copy(wo_ref, wo_all.at[lon], own_sems.at[1]),
        pltpu.make_async_copy(kv_ref, kv_own, own_sems.at[2]),
    ]
    for copy in own_copies:
        copy.start()

    z_peers = [lax.rem(z + d, n_z) * n_y + y for d in range(1, n_z)]
    y_peers = [z * n_y + lax.rem(y + d, n_y) for d in range(1, n_y)]
    barrier = pltpu.get_barrier_semaphore()
    for peer in z_peers + y_peers:
        pl.semaphore_signal(barrier, inc=1, device_id=(lat, peer), device_id_type=MESH)
    pl.semaphore_signal(barrier, inc=1, device_id=(mate, lon), device_id_type=MESH)

    @pl.when(has_far)
    def _():
        pl.semaphore_signal(barrier, inc=1, device_id=(far_safe, lon), device_id_type=MESH)

    pl.semaphore_wait(barrier, n_z - 1 + n_y - 1 + 1 + has_far.astype(jnp.int32))

    def wq_part(piece, half):
        return wq_all.at[pl.ds(pl.multiple_of(piece * depth + half * half_q, half_q), half_q)]

    def wo_part(piece, half):
        return wo_all.at[piece, pl.ds(pl.multiple_of(half * half_o, half_o), half_o)]

    wq_mine = wq_ref.at[pl.ds(pl.multiple_of(core * half_q, half_q), half_q)]
    wo_mine = wo_ref.at[pl.ds(pl.multiple_of(core * half_o, half_o), half_o)]
    w_query = (wq_part, wq_mine, wq_z, wq_y, wq_core, wq_recv)
    w_out = (wo_part, wo_mine, wo_z, wo_y, wo_core, wo_recv)

    def send_y(weight, piece_z, src):
        part, _, _, y_sems, _, recv = weight
        piece = piece_z * n_y + y
        for d, peer in enumerate(y_peers):
            remote(src, part(piece, core), y_sems.at[piece_z, d], recv.at[piece, core], (lat, peer)).start()

    def send_first(weight):
        part, mine, z_sems, _, _, recv = weight
        send_y(weight, z, mine)
        for d, peer in enumerate(z_peers):
            remote(mine, part(lon, core), z_sems.at[d], recv.at[lon, core], (lat, peer)).start()

    def arrived(weight, piece, half):
        part, _, _, _, core_sems, recv = weight
        ref = part(piece, half)
        remote(ref, ref, core_sems.at[piece], recv.at[piece, half], (mate, lon)).wait_recv()
        return ref

    def send_core(weight, piece, ref):
        part, _, _, _, core_sems, recv = weight
        remote(ref, part(piece, core), core_sems.at[piece], recv.at[piece, core], (mate, lon)).start()

    def pass_z(weight):
        for d in range(1, n_z):
            piece_z = lax.rem(z + n_z - d, n_z)
            piece = piece_z * n_y + y
            ref = arrived(weight, piece, core)
            send_y(weight, piece_z, ref)
            send_core(weight, piece, ref)

    def pass_y(weight):
        for k in range(n_z):
            piece_z = lax.rem(z + n_z - k, n_z)
            for d in range(1, n_y):
                piece = piece_z * n_y + lax.rem(y + n_y - d, n_y)
                send_core(weight, piece, arrived(weight, piece, core))

    def finish(weight):
        for d in range(1, n_lon):
            arrived(weight, lax.rem(lon + d, n_lon), 1 - core)

    def drain(weight):
        part, mine, z_sems, y_sems, core_sems, recv = weight
        for d, peer in enumerate(z_peers):
            remote(mine, part(lon, core), z_sems.at[d], recv.at[lon, core], (lat, peer)).wait_send()
        for k in range(n_z):
            for d, peer in enumerate(y_peers):
                remote(mine, part(lon, core), y_sems.at[k, d], recv.at[lon, core], (lat, peer)).wait_send()
        for d in range(1, n_lon):
            piece = lax.rem(lon + d, n_lon)
            remote(mine, part(lon, core), core_sems.at[piece], recv.at[lon, core], (mate, lon)).wait_send()

    def kv_copy(to_far, block, kind):
        target = kv_far if to_far else kv_chip
        index = (1 if to_far else 0, block, kind)
        return remote(
            kv_ref.at[kind, block], target.at[kind, block], kv_send.at[index], kv_recv.at[index],
            (far_safe if to_far else mate, lon),
        )

    send_first(w_query)
    for block in range(blocks):
        for kind in range(2):
            kv_copy(False, block, kind).start()

    @pl.when(has_far)
    def _():
        for block in range(blocks):
            for kind in range(2):
                kv_copy(True, block, kind).start()

    tokens = queries_ref[...].astype(jnp.float32)
    scale = lax.rsqrt(jnp.mean(tokens * tokens, axis=1, keepdims=True) + 1e-5)
    normed[...] = (tokens * scale * gain_ref[...].astype(jnp.float32)).astype(jnp.bfloat16)

    pass_z(w_query)
    pass_y(w_query)
    finish(w_query)
    send_first(w_out)
    own_copies[0].wait()

    lane = lax.broadcasted_iota(jnp.int32, (rows, PAIR), 1)

    @pl.loop(0, pairs // 2)
    def _(step):
        at = pl.multiple_of(step * 2 * PAIR, 2 * PAIR)
        made = jnp.dot(normed[...], wq_all[:, pl.ds(at, 2 * PAIR)], preferred_element_type=jnp.float32)
        made = made * HD ** (-0.5)
        for side in range(2):
            both = made[:, side * PAIR : (side + 1) * PAIR]
            heads[2 * step + side, :rows] = jnp.where(lane < HD, both, 0.0).astype(jnp.bfloat16)
            heads[2 * step + side, rows:] = jnp.where(lane < HD, 0.0, both).astype(jnp.bfloat16)

    def is_listed(block):
        found = jnp.logical_and(lists_ref[0, 0] == block, 0 < counts_ref[0])
        for slot in range(1, lists_ref.shape[1]):
            found = jnp.logical_or(
                found, jnp.logical_and(lists_ref[0, slot] == block, slot < counts_ref[0])
            )
        return found

    def attend(kv, band, which, first):
        live = [is_listed(band * blocks + b) for b in which]

        @pl.loop(0, pairs)
        def _(pair):
            at = pl.ds(pl.multiple_of(pair * PAIR, PAIR), PAIR)
            for part in range(2):
                here = pl.ds(part * rows, rows)
                q = heads[pair, here]
                scores = [
                    lax.dot_general(
                        q, kv[0, b, :, at], (((1,), (1,)), ((), ())), preferred_element_type=jnp.float32
                    )
                    for b in which
                ]
                peak = None if first else best[pair, here][:, :1]
                for s, alive in zip(scores, live):
                    top = jnp.where(alive, jnp.max(s, axis=1, keepdims=True), LOW)
                    peak = jnp.maximum(top, LOW) if peak is None else jnp.maximum(peak, top)
                added, mixed = None, None
                for s, alive, b in zip(scores, live, which):
                    weights = jnp.exp(s - jnp.where(alive, peak, jnp.inf))
                    lanes = weights[:, :128]
                    for k in range(1, BLOCK_TOKENS // 128):
                        lanes = lanes + weights[:, k * 128 : (k + 1) * 128]
                    product = jnp.dot(
                        weights.astype(jnp.bfloat16), kv[1, b, :, at], preferred_element_type=jnp.float32
                    )
                    added = lanes if added is None else added + lanes
                    mixed = product if mixed is None else mixed + product
                if first:
                    total[pair, here] = added
                    running[pair, here] = mixed
                else:
                    rescale = jnp.exp(best[pair, here][:, :1] - peak)
                    total[pair, here] = total[pair, here] * rescale + added
                    running[pair, here] = running[pair, here] * rescale + mixed
                best[pair, here] = jnp.broadcast_to(peak, (rows, PAIR))

    own_copies[2].wait()
    attend(kv_own, lat, range(blocks), True)
    pass_z(w_out)
    for block in range(blocks):
        for kind in range(2):
            kv_copy(False, block, kind).wait()
    attend(kv_chip, mate, range(blocks), False)
    pass_y(w_out)

    @pl.when(has_far)
    def _():
        for block in range(blocks):
            for kind in range(2):
                kv_copy(True, block, kind).wait()
            attend(kv_far, far_safe, [block], False)

    @pl.loop(0, pairs)
    def _(pair):
        at = pl.ds(pl.multiple_of(pair * PAIR, PAIR), PAIR)
        parts = []
        for part in range(2):
            here = pl.ds(part * rows, rows)
            parts.append(running[pair, here] / jnp.sum(total[pair, here], axis=1, keepdims=True))
        attended[:, at] = jnp.where(lane < HD, parts[0], parts[1]).astype(jnp.bfloat16)

    finish(w_out)
    own_copies[1].wait()
    group = max(1, 256 // columns)
    for step in range(n_lon // group):
        weight = jnp.concatenate([wo_all[step * group + k] for k in range(group)], axis=1)
        made = jnp.dot(attended[...], weight, preferred_element_type=jnp.float32)
        out_ref[:, step * group * columns : (step + 1) * group * columns] = made.astype(jnp.bfloat16)
    drain(w_query)
    drain(w_out)


def solution(mesh):
    n_lat, n_lon = mesh.shape["lat"], mesh.shape["lon"]
    n_y = 1
    while n_y * n_y * 4 <= n_lon:
        n_y *= 2
    n_z = n_lon // n_y

    def on_device(queries, gain, w_query, w_out, kv_cache, nbr_lists, counts):
        rows, width = queries.shape
        depth, columns = w_query.shape[0], w_out.shape[1]
        blocks = kv_cache.shape[1]
        vmem = pl.BlockSpec(memory_space=pltpu.VMEM)
        smem = pl.BlockSpec(memory_space=pltpu.SMEM)
        anywhere = pl.BlockSpec(memory_space=pl.ANY)
        dma = pltpu.SemaphoreType.DMA
        weight_sems = [dma((max(n_z - 1, 1),)), dma((n_z, max(n_y - 1, 1))), dma((n_lon,)), dma((n_lon, 2))]
        state = pltpu.VMEM((H // 2, 2 * rows, PAIR), jnp.float32)
        return pl.pallas_call(
            functools.partial(kernel, n_lat, n_z, n_y),
            out_shape=jax.ShapeDtypeStruct((rows, width), jnp.bfloat16),
            in_specs=[smem, smem, vmem, vmem, anywhere, anywhere, anywhere],
            out_specs=vmem,
            scratch_shapes=[
                pltpu.VMEM((width, width), jnp.bfloat16),
                pltpu.VMEM((n_lon, width, columns), jnp.bfloat16),
                pltpu.VMEM(kv_cache.shape, jnp.bfloat16),
                pltpu.VMEM(kv_cache.shape, jnp.bfloat16),
                pltpu.VMEM(kv_cache.shape, jnp.bfloat16),
                pltpu.VMEM((rows, width), jnp.bfloat16),
                pltpu.VMEM((H // 2, 2 * rows, PAIR), jnp.bfloat16),
                state,
                state,
                state,
                pltpu.VMEM((rows, width), jnp.bfloat16),
                dma((3,)),
                dma((2, blocks, 2)),
                dma((2, blocks, 2)),
                *weight_sems,
                *weight_sems,
            ],
            compiler_params=pltpu.CompilerParams(
                collective_id=0, has_side_effects=True, vmem_limit_bytes=48 * 1024 * 1024
            ),
        )(nbr_lists, counts, queries, gain.reshape(1, width), w_query, w_out, kv_cache)

    placed = (
        P(("lat", "lon"), None),
        P(),
        P("lon", None),
        P(None, "lon"),
        P(None, "lat", None, None),
        P(("lat", "lon"), None),
        P(("lat", "lon")),
    )
    return jax.shard_map(
        on_device, mesh=mesh, in_specs=placed, out_specs=P(("lat", "lon"), None), check_vma=False
    )
```

time: 124 us -> 68.8 us (0.55)
  Pallas kernels: 0 us -> 60.5 us
  waiting for transfers between devices: 53.5 us -> 0 us
  matrix products: 17 us -> 0 us
  between operations: 13.5 us -> 0.67 us
  loops' own time: 10.4 us -> 0 us
  local copies, waits for them, and re-layouts: 16.2 us -> 6.67 us
  starting transfers between devices: 6.47 us -> 0 us
  other arithmetic: 4.89 us -> 0 us
    pallas_call x0 -> x1, Pallas kernels: none -> 60.5 us  [on_device(): pl.pallas_call(functools.partial(kernel, n_lat, n_z, n_y), out_shape=jax....]
    all_gather x2 -> x0, waiting for transfers between devices: 31.6 us -> none  [the longest x1 23.3 us: on_device(): lax.all_gather(w_out, 'lon', axis=1, tiled=True)]
    ppermute x2 -> x0, waiting for transfers between devices: 21.2 us -> none  [the longest x1 18.7 us: padded(): before = lax.ppermute(last, axis, up)]
    dot_general x8 -> x0, matrix products: 17 us -> none  [the longest x3 5.93 us: update(): jnp.einsum(value_form, expo.astype(jnp.bfloat16), value_rows, preferred_e...]
    another operation x1 -> x0, loops' own time: 10.4 us -> none  [on_device(): final_state = lax.fori_loop(0, jnp.max(counts), listed_step, start_state)]
    slice x3 -> x0, local copies, waits for them, and re-layouts: 10.2 us -> none  [the longest x2 5.54 us: on_device(): value_window = window[1].reshape(3 * blocks_here, BLOCK_TOKENS, H, HD)]
    ppermute x2 -> x0, starting transfers between devices: 6.43 us -> none  [the longest x1 4.51 us: padded(): before = lax.ppermute(last, axis, up)]
    unnamed x4 -> x11, local copies, waits for them, and re-layouts: 1.94 us -> 5.98 us
  transfers between devices with their start and end apart: 4 -> 0, of which waited for: 4 -> 0; matrix products, arithmetic and copies ran while one was open for 29% -> 0% of each run, Pallas kernels for 0% -> 0%
where the time goes in v1:
time: 68.8 us; the launch traced here: 67.8 us
  Pallas kernels  60.5 us (88%)
  local copies, waits for them, and re-layouts  6.67 us (10%)
    pallas_call x1, Pallas kernels, on_device(): pl.pallas_call(functools.partial(kernel, n_lat, n_z, n_y), out_shape=jax....  60.5 us
    unnamed x11, local copies, waits for them, and re-layouts  5.98 us

profile of v1, /device:TPU:1, one launch (start us, length us, event | category | flops | bytes accessed | tf_op | source)
XLA Modules:
  0.0 67.8 jit_solution(16965497947860429395)
XLA Ops:
  0.7 0.7 %reshape.3.gain_ref = bf16[1,1024]{1,0:T(2,128)(2,1)S(1)} reshape(bf16[1024]{0:T(1024)(128)(2,1)} %param.8) | data formatting | bytes 4096 | tf_op jit(solution)/shard_map/reshape | solution.py:295
  1.3 0.0 copy-start
  1.3 1.6 %copy-done = bf16[2,2,256,1024]{3,2,1,0:T(8,128)(2,1)S(1)} copy-done((bf16[2,2,256,1024]{3,2,1,0:T(8,128)(2,1)S(1)}, bf16[2,2,256,1024]{3,2,1,0:T(8,128)(2,1)}, u32[]{:S(2)}) %copy-start) | copy-done | bytes 2097176
  2.9 0.0 copy-start.1
  2.9 1.0 %copy-done.1 = bf16[256,1024]{1,0:T(8,128)(2,1)S(1)} copy-done((bf16[256,1024]{1,0:T(8,128)(2,1)S(1)}, bf16[256,1024]{1,0:T(8,128)(2,1)}, u32[]{:S(2)}) %copy-start.1) | copy-done | bytes 524312
  4.0 0.0 copy-start.2
  4.0 0.9 %copy-done.2 = bf16[128,1024]{1,0:T(8,128)(2,1)S(1)} copy-done((bf16[128,1024]{1,0:T(8,128)(2,1)S(1)}, bf16[128,1024]{1,0:T(8,128)(2,1)}, u32[]{:S(2)}) %copy-start.2) | copy-done | bytes 262168
  4.9 0.0 copy-start.3
  4.9 0.9 %copy-done.3 = bf16[1024,128]{1,0:T(8,128)(2,1)S(1)} copy-done((bf16[1024,128]{1,0:T(8,128)(2,1)S(1)}, bf16[1024,128]{1,0:T(8,128)(2,1)}, u32[]{:S(2)}) %copy-start.3) | copy-done | bytes 262168
  5.9 0.0 copy-start.4
  5.9 0.7 copy-done.4
  6.5 60.5 %shard_map.73 = bf16[256,1024]{1,0:T(8,128)(2,1)S(1)} custom-call(s32[1,4]{1,0:T(1,128)S(1)} %copy-done.4, s32[1]{0:T(128)S(6)} %copy.9.counts_ref, bf16[256,1024]{1,0:T(8,128)(2,1)S(1)} %copy-done.1, bf16[1,1024]{1,0:T(2,128)(2,1)S(1)} %reshape.3.gain_ref, bf16[128,1024]{1,0:T(8,128)(2,1)S(1)} %copy-done.2, bf16[1024,128]{1,0:T(8,128)(2,1)S(1)} %copy-done.3, ...), custom_call_target="tpu_custom_call" | custom-call | tf_op jit(solution)/shard_map/pallas_call | solution.py:269
  67.0 0.8 %copy.10 = bf16[256,1024]{1,0:T(8,128)(2,1)} copy(bf16[256,1024]{1,0:T(8,128)(2,1)S(1)} %shard_map.73) | data formatting | bytes 1048576
Async XLA Ops:
  1.3 1.6 %copy-start = (bf16[2,2,256,1024]{3,2,1,0:T(8,128)(2,1)S(1)}, bf16[2,2,256,1024]{3,2,1,0:T(8,128)(2,1)}, u32[]{:S(2)}) copy-start(bf16[2,2,256,1024]{3,2,1,0:T(8,128)(2,1)} %kv_ref.1) | copy-start | bytes 6291460
  2.9 1.0 %copy-start.1 = (bf16[256,1024]{1,0:T(8,128)(2,1)S(1)}, bf16[256,1024]{1,0:T(8,128)(2,1)}, u32[]{:S(2)}) copy-start(bf16[256,1024]{1,0:T(8,128)(2,1)} %queries_ref.1) | copy-start | bytes 1572868
  4.0 0.9 %copy-start.2 = (bf16[128,1024]{1,0:T(8,128)(2,1)S(1)}, bf16[128,1024]{1,0:T(8,128)(2,1)}, u32[]{:S(2)}) copy-start(bf16[128,1024]{1,0:T(8,128)(2,1)} %wq_ref.1) | copy-start | bytes 786436
  4.9 0.9 %copy-start.3 = (bf16[1024,128]{1,0:T(8,128)(2,1)S(1)}, bf16[1024,128]{1,0:T(8,128)(2,1)}, u32[]{:S(2)}) copy-start(bf16[1024,128]{1,0:T(8,128)(2,1)} %wo_ref.1) | copy-start | bytes 786436
  5.9 0.7 copy-start.4

commit v2 on v1

v2 whole, which is shorter than its diff:
```python
import functools

import jax
import jax.numpy as jnp
from jax import lax
from jax.experimental import pallas as pl
from jax.experimental.pallas import tpu as pltpu
from jax.sharding import PartitionSpec as P

H = 16
HD = 64
PAIR = 2 * HD
BLOCK_TOKENS = 256
MESH = pl.DeviceIdType.MESH
LOW = -1e30


def remote(src, dst, send_sem, recv_sem, device):
    return pltpu.make_async_remote_copy(
        src_ref=src, dst_ref=dst, send_sem=send_sem, recv_sem=recv_sem, device_id=device, device_id_type=MESH
    )


def kernel(
    n_lat, n_z, n_y,
    lists_hbm, counts_hbm, queries_hbm, gain_hbm, wq_ref, wo_ref, kv_ref,
    out_ref,
    lists_ref, counts_ref, queries_ref, gain_ref, wq_all, wo_all, kv_own, kv_chip, kv_far, normed, heads, best, total, running, attended,
    own_sems, kv_send, kv_recv, wq_z, wq_y, wq_core, wq_recv, wo_z, wo_y, wo_core, wo_recv,
):
    n_lon = n_z * n_y
    lat, lon = lax.axis_index("lat"), lax.axis_index("lon")
    z, y, core = lon // n_y, lon % n_y, lat % 2
    mate = lat + 1 - 2 * core
    far = lat - 1 + 2 * core
    has_far = jnp.logical_and(far >= 0, far < n_lat)
    far_safe = jnp.clip(far, 0, n_lat - 1)
    pairs = H // 2
    rows = queries_ref.shape[0]
    depth, columns = wq_ref.shape[0], wo_ref.shape[1]
    half_q, half_o = depth // 2, wo_ref.shape[0] // 2
    blocks = kv_ref.shape[1]

    own_copies = [
        pltpu.make_async_copy(wq_ref, wq_all.at[pl.ds(pl.multiple_of(lon * depth, depth), depth)], own_sems.at[0]),
        pltpu.make_async_copy(wo_ref, wo_all.at[lon], own_sems.at[1]),
        pltpu.make_async_copy(kv_ref, kv_own, own_sems.at[2]),
        pltpu.make_async_copy(queries_hbm, queries_ref, own_sems.at[3]),
        pltpu.make_async_copy(gain_hbm, gain_ref, own_sems.at[4]),
        pltpu.make_async_copy(lists_hbm, lists_ref, own_sems.at[5]),
        pltpu.make_async_copy(counts_hbm, counts_ref, own_sems.at[6]),
    ]
    for copy in own_copies:
        copy.start()

    above, below = z + 1 < n_z, z > 0
    lon_up, lon_down = jnp.minimum(lon + n_y, n_lon - 1), jnp.maximum(lon - n_y, 0)
    y_peers = [z * n_y + lax.rem(y + d, n_y) for d in range(1, n_y)]
    barrier = pltpu.get_barrier_semaphore()
    for there, peer in ((above, lon_up), (below, lon_down)):

        @pl.when(there)
        def _(peer=peer):
            pl.semaphore_signal(barrier, inc=1, device_id=(lat, peer), device_id_type=MESH)

    for peer in y_peers:
        pl.semaphore_signal(barrier, inc=1, device_id=(lat, peer), device_id_type=MESH)
    pl.semaphore_signal(barrier, inc=1, device_id=(mate, lon), device_id_type=MESH)

    @pl.when(has_far)
    def _():
        pl.semaphore_signal(barrier, inc=1, device_id=(far_safe, lon), device_id_type=MESH)

    pl.semaphore_wait(barrier, n_y + sum(there.astype(jnp.int32) for there in (has_far, above, below)))

    def wq_part(piece, half):
        return wq_all.at[pl.ds(pl.multiple_of(piece * depth + half * half_q, half_q), half_q)]

    def wo_part(piece, half):
        return wo_all.at[piece, pl.ds(pl.multiple_of(half * half_o, half_o), half_o)]

    wq_mine = wq_ref.at[pl.ds(pl.multiple_of(core * half_q, half_q), half_q)]
    wo_mine = wo_ref.at[pl.ds(pl.multiple_of(core * half_o, half_o), half_o)]
    w_query = (wq_part, wq_mine, wq_z, wq_y, wq_core, wq_recv)
    w_out = (wo_part, wo_mine, wo_z, wo_y, wo_core, wo_recv)

    def send_y(weight, piece_z, src):
        part, _, _, y_sems, _, recv = weight
        piece = piece_z * n_y + y
        for d, peer in enumerate(y_peers):
            remote(src, part(piece, core), y_sems.at[piece_z, d], recv.at[piece, core], (lat, peer)).start()

    def z_copy(weight, piece_z, src, up):
        part, _, z_sems, _, _, recv = weight
        piece = piece_z * n_y + y
        peer = lon_up if up else lon_down
        return remote(
            src, part(piece, core), z_sems.at[piece_z, 0 if up else 1], recv.at[piece, core], (lat, peer)
        )

    def send_first(weight):
        mine = weight[1]

        @pl.when(above)
        def _():
            z_copy(weight, z, mine, True).start()

        @pl.when(below)
        def _():
            z_copy(weight, z, mine, False).start()

        send_y(weight, z, mine)

    def arrived(weight, piece, half):
        part, _, _, _, core_sems, recv = weight
        ref = part(piece, half)
        remote(ref, ref, core_sems.at[piece], recv.at[piece, half], (mate, lon)).wait_recv()
        return ref

    def send_core(weight, piece, ref):
        part, _, _, _, core_sems, recv = weight
        remote(ref, part(piece, core), core_sems.at[piece], recv.at[piece, core], (mate, lon)).start()

    def pass_z(weight):
        for d in range(1, n_z):
            for up, piece_z, there in ((True, z - d, z >= d), (False, z + d, z + d < n_z)):

                @pl.when(there)
                def _(up=up, piece_z=piece_z):
                    piece = piece_z * n_y + y
                    ref = arrived(weight, piece, core)

                    @pl.when(above if up else below)
                    def _():
                        z_copy(weight, piece_z, ref, up).start()

                    send_y(weight, piece_z, ref)
                    send_core(weight, piece, ref)

    def pass_y(weight):
        def pass_one(piece_z):
            for d in range(1, n_y):
                piece = piece_z * n_y + lax.rem(y + n_y - d, n_y)
                send_core(weight, piece, arrived(weight, piece, core))

        pass_one(z)
        for d in range(1, n_z):
            for piece_z, there in ((z - d, z >= d), (z + d, z + d < n_z)):

                @pl.when(there)
                def _(piece_z=piece_z):
                    pass_one(piece_z)

    def finish(weight):
        for d in range(1, n_lon):
            arrived(weight, lax.rem(lon + d, n_lon), 1 - core)

    def drain(weight):
        part, mine, z_sems, y_sems, core_sems, recv = weight
        for piece_z in range(n_z):

            @pl.when(jnp.logical_and(above, piece_z <= z))
            def _(piece_z=piece_z):
                z_copy(weight, piece_z, mine, True).wait_send()

            @pl.when(jnp.logical_and(below, piece_z >= z))
            def _(piece_z=piece_z):
                z_copy(weight, piece_z, mine, False).wait_send()

        for k in range(n_z):
            for d, peer in enumerate(y_peers):
                remote(mine, part(lon, core), y_sems.at[k, d], recv.at[lon, core], (lat, peer)).wait_send()
        for d in range(1, n_lon):
            piece = lax.rem(lon + d, n_lon)
            remote(mine, part(lon, core), core_sems.at[piece], recv.at[lon, core], (mate, lon)).wait_send()

    def kv_copy(to_far, block, kind):
        target = kv_far if to_far else kv_chip
        index = (1 if to_far else 0, block, kind)
        return remote(
            kv_ref.at[kind, block], target.at[kind, block], kv_send.at[index], kv_recv.at[index],
            (far_safe if to_far else mate, lon),
        )

    send_first(w_query)
    for block in range(blocks):
        for kind in range(2):
            kv_copy(False, block, kind).start()

    @pl.when(has_far)
    def _():
        for block in range(blocks):
            for kind in range(2):
                kv_copy(True, block, kind).start()

    own_copies[3].wait()
    own_copies[4].wait()
    tokens = queries_ref[...].astype(jnp.float32)
    scale = lax.rsqrt(jnp.mean(tokens * tokens, axis=1, keepdims=True) + 1e-5)
    normed[...] = (tokens * scale * gain_ref[...].astype(jnp.float32)).astype(jnp.bfloat16)

    pass_z(w_query)
    send_first(w_out)
    pass_y(w_query)
    finish(w_query)
    own_copies[0].wait()

    feature = lax.broadcasted_iota(jnp.int32, (PAIR, rows), 0)

    @pl.loop(0, pairs // 2)
    def _(step):
        at = pl.multiple_of(step * 2 * PAIR, 2 * PAIR)
        made = jnp.dot(normed[...], wq_all[:, pl.ds(at, 2 * PAIR)], preferred_element_type=jnp.float32)
        made = (made * HD ** (-0.5)).T
        for side in range(2):
            both = made[side * PAIR : (side + 1) * PAIR]
            heads[2 * step + side, :, :rows] = jnp.where(feature < HD, both, 0.0).astype(jnp.bfloat16)
            heads[2 * step + side, :, rows:] = jnp.where(feature < HD, 0.0, both).astype(jnp.bfloat16)

    own_copies[5].wait()
    own_copies[6].wait()

    def is_listed(block):
        found = jnp.logical_and(lists_ref[0, 0] == block, 0 < counts_ref[0])
        for slot in range(1, lists_ref.shape[1]):
            found = jnp.logical_or(
                found, jnp.logical_and(lists_ref[0, slot] == block, slot < counts_ref[0])
            )
        return found

    def attend(kv, band, first):
        live = [is_listed(band * blocks + b) for b in range(blocks)]

        @pl.loop(0, pairs)
        def _(pair):
            at = pl.ds(pl.multiple_of(pair * PAIR, PAIR), PAIR)
            values = [kv[1, b, :, at].T for b in range(blocks)]
            for part in range(2):
                q = heads[pair, :, part * rows : (part + 1) * rows]
                own = pl.ds(part * HD, HD)
                one = pl.ds(part, 1)
                scores = [
                    jnp.dot(kv[0, b, :, at], q, preferred_element_type=jnp.float32) for b in range(blocks)
                ]
                peak = jnp.full((1, rows), LOW, jnp.float32) if first else best[pair, one]
                for s, alive in zip(scores, live):
                    peak = jnp.maximum(peak, jnp.where(alive, jnp.max(s, axis=0, keepdims=True), LOW))
                added, mixed = 0.0, 0.0
                for s, alive, value in zip(scores, live, values):
                    weights = jnp.exp(s - jnp.where(alive, peak, jnp.inf))
                    added = added + jnp.sum(weights, axis=0, keepdims=True)
                    mixed = mixed + jnp.dot(
                        value[part * HD : (part + 1) * HD],
                        weights.astype(jnp.bfloat16),
                        preferred_element_type=jnp.float32,
                    )
                if not first:
                    rescale = jnp.exp(best[pair, one] - peak)
                    added = added + total[pair, one] * rescale
                    mixed = mixed + running[pair, own] * rescale
                best[pair, one] = peak
                total[pair, one] = added
                running[pair, own] = mixed

    own_copies[2].wait()
    attend(kv_own, lat, True)
    pass_z(w_out)
    for block in range(blocks):
        for kind in range(2):
            kv_copy(False, block, kind).wait()
    attend(kv_chip, mate, False)
    pass_y(w_out)

    @pl.when(has_far)
    def _():
        for block in range(blocks):
            for kind in range(2):
                kv_copy(True, block, kind).wait()
        attend(kv_far, far_safe, False)

    @pl.loop(0, pairs)
    def _(pair):
        at = pl.ds(pl.multiple_of(pair * PAIR, PAIR), PAIR)
        over = jnp.where(feature < HD, total[pair, 0:1], total[pair, 1:2])
        attended[:, at] = (running[pair] / over).T.astype(jnp.bfloat16)

    finish(w_out)
    own_copies[1].wait()
    group = max(1, 256 // columns)
    for step in range(n_lon // group):
        weight = jnp.concatenate([wo_all[step * group + k] for k in range(group)], axis=1)
        made = jnp.dot(attended[...], weight, preferred_element_type=jnp.float32)
        out_ref[:, step * group * columns : (step + 1) * group * columns] = made.astype(jnp.bfloat16)
    drain(w_query)
    drain(w_out)


def solution(mesh):
    n_lat, n_lon = mesh.shape["lat"], mesh.shape["lon"]
    n_y = 1
    while n_y * n_y * 4 <= n_lon:
        n_y *= 2
    n_z = n_lon // n_y

    def on_device(queries, gain, w_query, w_out, kv_cache, nbr_lists, counts):
        rows, width = queries.shape
        depth, columns = w_query.shape[0], w_out.shape[1]
        blocks = kv_cache.shape[1]
        vmem = pl.BlockSpec(memory_space=pltpu.VMEM)
        anywhere = pl.BlockSpec(memory_space=pltpu.HBM)
        dma = pltpu.SemaphoreType.DMA
        weight_sems = [dma((n_z, 2)), dma((n_z, max(n_y - 1, 1))), dma((n_lon,)), dma((n_lon, 2))]
        state = pltpu.VMEM((H // 2, 8, rows), jnp.float32)
        return pl.pallas_call(
            functools.partial(kernel, n_lat, n_z, n_y),
            out_shape=jax.ShapeDtypeStruct((rows, width), jnp.bfloat16),
            in_specs=[anywhere] * 7,
            out_specs=vmem,
            scratch_shapes=[
                pltpu.SMEM(nbr_lists.shape, jnp.int32),
                pltpu.SMEM(counts.shape, jnp.int32),
                pltpu.VMEM((rows, width), jnp.bfloat16),
                pltpu.VMEM((1, width), jnp.bfloat16),
                pltpu.VMEM((width, width), jnp.bfloat16),
                pltpu.VMEM((n_lon, width, columns), jnp.bfloat16),
                pltpu.VMEM(kv_cache.shape, jnp.bfloat16),
                pltpu.VMEM(kv_cache.shape, jnp.bfloat16),
                pltpu.VMEM(kv_cache.shape, jnp.bfloat16),
                pltpu.VMEM((rows, width), jnp.bfloat16),
                pltpu.VMEM((H // 2, PAIR, 2 * rows), jnp.bfloat16),
                state,
                state,
                pltpu.VMEM((H // 2, PAIR, rows), jnp.float32),
                pltpu.VMEM((rows, width), jnp.bfloat16),
                dma((7,)),
                dma((2, blocks, 2)),
                dma((2, blocks, 2)),
                *weight_sems,
                *weight_sems,
            ],
            compiler_params=pltpu.CompilerParams(
                collective_id=0, has_side_effects=True, vmem_limit_bytes=48 * 1024 * 1024
            ),
        )(nbr_lists, counts, queries, gain.reshape(1, width), w_query, w_out, kv_cache)

    placed = (
        P(("lat", "lon"), None),
        P(),
        P("lon", None),
        P(None, "lon"),
        P(None, "lat", None, None),
        P(("lat", "lon"), None),
        P(("lat", "lon")),
    )
    return jax.shard_map(
        on_device, mesh=mesh, in_specs=placed, out_specs=P(("lat", "lon"), None), check_vma=False
    )
```

time: 68.8 us -> 62.3 us (0.906)
  Pallas kernels: 60.5 us -> 54.6 us
    pallas_call x1, Pallas kernels: 60.5 us -> 54.6 us  [on_device(): pl.pallas_call(functools.partial(kernel, n_lat, n_z, n_y), out_shape=jax....]
where the time goes in v2:
time: 62.3 us; the launch traced here: 62 us
  Pallas kernels  54.6 us (88%)
  local copies, waits for them, and re-layouts  6.67 us (11%)
  between operations  0.67 us (1%)
    pallas_call x1, Pallas kernels, on_device(): pl.pallas_call(functools.partial(kernel, n_lat, n_z, n_y), out_shape=jax....  54.6 us
    unnamed x11, local copies, waits for them, and re-layouts  5.98 us

profile of v2, /device:TPU:1, one launch (start us, length us, event | category | flops | bytes accessed | tf_op | source)
XLA Modules:
  0.0 62.0 jit_solution(7916097948565840104)
XLA Ops:
  0.7 0.7 %reshape.3.gain_hbm = bf16[1,1024]{1,0:T(2,128)(2,1)S(1)} reshape(bf16[1024]{0:T(1024)(128)(2,1)} %param.8) | data formatting | bytes 4096 | tf_op jit(solution)/shard_map/reshape | solution.py:344
  1.3 0.0 copy-start
  1.3 1.6 %copy-done = bf16[2,2,256,1024]{3,2,1,0:T(8,128)(2,1)S(1)} copy-done((bf16[2,2,256,1024]{3,2,1,0:T(8,128)(2,1)S(1)}, bf16[2,2,256,1024]{3,2,1,0:T(8,128)(2,1)}, u32[]{:S(2)}) %copy-start) | copy-done | bytes 2097176
  2.9 0.0 copy-start.1
  2.9 1.0 %copy-done.1 = bf16[256,1024]{1,0:T(8,128)(2,1)S(1)} copy-done((bf16[256,1024]{1,0:T(8,128)(2,1)S(1)}, bf16[256,1024]{1,0:T(8,128)(2,1)}, u32[]{:S(2)}) %copy-start.1) | copy-done | bytes 524312
  4.0 0.0 copy-start.2
  4.0 0.9 %copy-done.2 = bf16[128,1024]{1,0:T(8,128)(2,1)S(1)} copy-done((bf16[128,1024]{1,0:T(8,128)(2,1)S(1)}, bf16[128,1024]{1,0:T(8,128)(2,1)}, u32[]{:S(2)}) %copy-start.2) | copy-done | bytes 262168
  4.9 0.0 copy-start.3
  4.9 0.9 %copy-done.3 = bf16[1024,128]{1,0:T(8,128)(2,1)S(1)} copy-done((bf16[1024,128]{1,0:T(8,128)(2,1)S(1)}, bf16[1024,128]{1,0:T(8,128)(2,1)}, u32[]{:S(2)}) %copy-start.3) | copy-done | bytes 262168
  5.9 0.0 copy-start.4
  5.9 0.7 %copy-done.4 = s32[1,4]{1,0:T(1,128)S(1)} copy-done((s32[1,4]{1,0:T(1,128)S(1)}, s32[1,4]{1,0:T(1,128)}, u32[]{:S(2)}) %copy-start.4) | copy-done | bytes 40
  6.5 54.6 %shard_map.73 = bf16[256,1024]{1,0:T(8,128)(2,1)S(1)} custom-call(s32[1,4]{1,0:T(1,128)S(1)} %copy-done.4, s32[1]{0:T(128)S(6)} %copy.9.counts_hbm, bf16[256,1024]{1,0:T(8,128)(2,1)S(1)} %copy-done.1, bf16[1,1024]{1,0:T(2,128)(2,1)S(1)} %reshape.3.gain_hbm, bf16[128,1024]{1,0:T(8,128)(2,1)S(1)} %copy-done.2, bf16[1024,128]{1,0:T(8,128)(2,1)S(1)} %copy-done.3, ...), custom_call_target="tpu_custom_call" | custom-call | tf_op jit(solution)/shard_map/pallas_call | solution.py:314
  61.2 0.8 %copy.10 = bf16[256,1024]{1,0:T(8,128)(2,1)} copy(bf16[256,1024]{1,0:T(8,128)(2,1)S(1)} %shard_map.73) | data formatting | bytes 1048576
Async XLA Ops:
  1.3 1.6 %copy-start = (bf16[2,2,256,1024]{3,2,1,0:T(8,128)(2,1)S(1)}, bf16[2,2,256,1024]{3,2,1,0:T(8,128)(2,1)}, u32[]{:S(2)}) copy-start(bf16[2,2,256,1024]{3,2,1,0:T(8,128)(2,1)} %kv_ref.1) | copy-start | bytes 6291460
  2.9 1.0 %copy-start.1 = (bf16[256,1024]{1,0:T(8,128)(2,1)S(1)}, bf16[256,1024]{1,0:T(8,128)(2,1)}, u32[]{:S(2)}) copy-start(bf16[256,1024]{1,0:T(8,128)(2,1)} %queries_hbm.1) | copy-start | bytes 1572868
  4.0 0.9 %copy-start.2 = (bf16[128,1024]{1,0:T(8,128)(2,1)S(1)}, bf16[128,1024]{1,0:T(8,128)(2,1)}, u32[]{:S(2)}) copy-start(bf16[128,1024]{1,0:T(8,128)(2,1)} %wq_ref.1) | copy-start | bytes 786436
  4.9 0.9 %copy-start.3 = (bf16[1024,128]{1,0:T(8,128)(2,1)S(1)}, bf16[1024,128]{1,0:T(8,128)(2,1)}, u32[]{:S(2)}) copy-start(bf16[1024,128]{1,0:T(8,128)(2,1)} %wo_ref.1) | copy-start | bytes 786436
  5.9 0.7 %copy-start.4 = (s32[1,4]{1,0:T(1,128)S(1)}, s32[1,4]{1,0:T(1,128)}, u32[]{:S(2)}) copy-start(s32[1,4]{1,0:T(1,128)} %lists_hbm.1) | copy-start | bytes 52

commit v3 on v2

--- a/solution.py
+++ b/solution.py
@@ -231,7 +231,7 @@
     def attend(kv, band, first):
         live = [is_listed(band * blocks + b) for b in range(blocks)]
 
-        @pl.loop(0, pairs)
+        @pl.loop(0, pairs, unroll=4)
         def _(pair):
             at = pl.ds(pl.multiple_of(pair * PAIR, PAIR), PAIR)
             values = [kv[1, b, :, at].T for b in range(blocks)]
@@ -263,13 +263,13 @@
                 running[pair, own] = mixed
 
     own_copies[2].wait()
+    pass_z(w_out)
     attend(kv_own, lat, True)
-    pass_z(w_out)
+    pass_y(w_out)
     for block in range(blocks):
         for kind in range(2):
             kv_copy(False, block, kind).wait()
     attend(kv_chip, mate, False)
-    pass_y(w_out)
 
     @pl.when(has_far)
     def _():
@@ -339,7 +339,7 @@
                 *weight_sems,
             ],
             compiler_params=pltpu.CompilerParams(
-                collective_id=0, has_side_effects=True, vmem_limit_bytes=48 * 1024 * 1024
+                collective_id=0, has_side_effects=True, vmem_limit_bytes=60 * 1024 * 1024
             ),
         )(nbr_lists, counts, queries, gain.reshape(1, width), w_query, w_out, kv_cache)
 

time: 62.3 us -> 56.9 us (0.913)
  local copies, waits for them, and re-layouts: 6.67 us -> 3.15 us
  Pallas kernels: 54.6 us -> 52.9 us
    unnamed x11 -> x1, local copies, waits for them, and re-layouts: 5.98 us -> 1.87 us
    pallas_call x1, Pallas kernels: 54.6 us -> 52.9 us  [on_device(): pl.pallas_call(functools.partial(kernel, n_lat, n_z, n_y), out_shape=jax....]
where the time goes in v3:
time: 56.9 us; the launch traced here: 56.7 us
  Pallas kernels  52.9 us (93%)
  local copies, waits for them, and re-layouts  3.15 us (6%)
  between operations  0.66 us (1%)
    pallas_call x1, Pallas kernels, on_device(): pl.pallas_call(functools.partial(kernel, n_lat, n_z, n_y), out_shape=jax....  52.9 us
    unnamed x1, local copies, waits for them, and re-layouts  1.87 us
    reshape x1, local copies, waits for them, and re-layouts, on_device(): gain.reshape(1, width)  1.28 us

profile of v3, /device:TPU:1, one launch (start us, length us, event | category | flops | bytes accessed | tf_op | source)
XLA Modules:
  0.0 56.7 jit_solution(10876173133998540021)
XLA Ops:
  0.7 1.3 %reshape.3.gain_hbm = bf16[1,1024]{1,0:T(2,128)(2,1)} reshape(bf16[1024]{0:T(1024)(128)(2,1)} %param.8) | data formatting | bytes 4096 | tf_op jit(solution)/shard_map/reshape | solution.py:344
  1.9 52.9 %shard_map.73 = bf16[256,1024]{1,0:T(8,128)(2,1)} custom-call(s32[1,4]{1,0:T(1,128)} %lists_hbm.1, s32[1]{0:T(128)S(6)} %copy.9.counts_hbm, bf16[256,1024]{1,0:T(8,128)(2,1)} %queries_hbm.1, bf16[1,1024]{1,0:T(2,128)(2,1)} %reshape.3.gain_hbm, bf16[128,1024]{1,0:T(8,128)(2,1)} %wq_ref.1, bf16[1024,128]{1,0:T(8,128)(2,1)} %wo_ref.1, ...), custom_call_target="tpu_custom_call" | custom-call | tf_op jit(solution)/shard_map/pallas_call | solution.py:314
  54.8 1.9 %copy.10 = bf16[256,1024]{1,0:T(8,128)(2,1)} copy(bf16[256,1024]{1,0:T(8,128)(2,1)} %shard_map.73) | data formatting | bytes 1048576
